TPU v7x, 512 devices: a whole 4x8x8 slice. The times are simulated.
512 devices in a mesh: col: 128 (over y_lo, z, x, core), row: 4 (over y_hi).
Axes of the slice: x: 4, y: 8 (y_hi: 4, y_lo: 2; y = y_hi * 2 + y_lo), z: 8, core: 2. Of those that a mesh axis runs over, the one named last changes fastest.
Arguments:
- g2_block: bfloat16 [2048, 2, 131072], P('row', None, 'col'), may hold values from -6 to 6
- panel_slots: bfloat16 [128, 2, 2, 256, 2048], P('col', None, None, None, 'row'), may hold values from -0.125 to 0.125
- owners: int32 [2], replicated, may hold values from 0 to 127
- green_one: float32 [2, 400, 400], replicated, may hold values from -6 to 6
Outputs:
- rate: bfloat16 [256, 2, 2, 131072], P('row', None, None, 'col')
All inputs are finite; a program needn't handle non-finite values.
Results may differ from a plain program's by a relative error of at most 0.012.
Values may be sent and summed in bfloat16 or wider, within the bound.
No kernel may reach another device: no remote copies, remote signals or barrier semaphores. Data moves between devices by JAX's collectives and lax.ppermute only.
A program may use at most 64 MiB of HBM per device.

v0:
```python
import jax
import jax.numpy as jnp
from jax import lax
from jax.sharding import Mesh, PartitionSpec as P

NPAN = 2
SIZES = {"y": 2, "z": 8, "x": 4, "core": 2, "row": 4}
COL = ("y", "z", "x", "core")


def pick(array, index):
    return lax.dynamic_index_in_dim(array, index, 0, keepdims=False)


def shift(array, step):
    size = SIZES["row"]
    return lax.ppermute(array, "row", [(index, (index + step) % size) for index in range(size)])


def spread_pieces(panel):
    half = panel.shape[-1] // 2
    pieces = panel.reshape(-1, 8, 2, half).transpose(0, 2, 1, 3).reshape(-1, 8, half)
    return lax.all_to_all(pieces, COL, 0, 0, tiled=True)


def gather(pieces):
    count = SIZES["y"] * SIZES["z"] * SIZES["x"]
    copies = jnp.broadcast_to(pieces[None], (count,) + pieces.shape)
    own = lax.all_to_all(copies, ("y", "z", "x"), 0, 0, tiled=True)
    other = lax.ppermute(own, "core", [(0, 1), (1, 0)])
    return [half.transpose(1, 0, 2, 3).reshape(NPAN, -1, half.shape[-1]) for half in (own, other)]


def turned(panel):
    re, im = panel.reshape(2, -1, panel.shape[-1])
    full = jnp.stack([jnp.concatenate([im, re], axis=1), jnp.concatenate([-re, im], axis=1)])
    full = full.reshape(2, SIZES["row"], -1, full.shape[-1]).transpose(1, 0, 2, 3)
    return full.reshape(SIZES["row"], -1, full.shape[-1])


def reduce_row(lefts, right):
    row = lax.axis_index("row")

    def term(index, step):
        left = pick(lefts[index], (row + step) % SIZES["row"])
        return jnp.dot(left, right, preferred_element_type=jnp.float32).astype(jnp.bfloat16)

    def with_term(array, index, step):
        return (array.astype(jnp.float32) + term(index, step).astype(jnp.float32)).astype(jnp.bfloat16)

    far = lax.optimization_barrier([shift(term(0, 2), 1), shift(term(1, 2), -1)])
    straight = [shift(term(0, 3), -1), shift(term(1, 1), 1)]
    sent = [with_term(far[0], 0, 1), with_term(far[1], 1, 3)]
    joined = [shift(sent[0], 1), shift(sent[1], -1)]
    own = [term(index, 0) for index in range(NPAN)]
    sums = [
        own[index].astype(jnp.float32) + straight[index].astype(jnp.float32) + joined[index].astype(jnp.float32)
        for index in range(NPAN)
    ]
    return sums, sent


def chosen(index, count):
    return (index[:, None] == jnp.arange(count, dtype=jnp.int32)[None, :]).astype(jnp.float32)


def source(owners, green, rows, width):
    orbitals = green.shape[1]
    first = (2 * owners + jnp.arange(NPAN, dtype=jnp.int32)) * (rows * SIZES["row"])
    pairs = first[:, None] + lax.axis_index("row") * rows + jnp.arange(rows, dtype=jnp.int32)[None, :]
    pairs = pairs.reshape(-1)
    columns = lax.axis_index(COL) * width + jnp.arange(width, dtype=jnp.int32)

    def take(row_index, col_index):
        half = jnp.einsum("qi,cik->cqk", chosen(row_index, orbitals), green, precision="highest")
        return jnp.einsum("cqk,nk->cqn", half, chosen(col_index, orbitals), precision="highest")

    a = take(pairs // orbitals, columns // orbitals)
    b = take(pairs % orbitals, columns % orbitals)
    re = a[0] * b[0] - a[1] * b[1]
    im = a[0] * b[1] + a[1] * b[0]
    return jnp.stack([re, im]).reshape(2, NPAN, rows, width).transpose(1, 0, 2, 3)


def shards(g2_block, panel_slots, owners, green_one):
    depth, _, width = g2_block.shape
    rows = panel_slots.shape[3] // SIZES["row"]
    core = lax.axis_index("core")
    panels = panel_slots[0].reshape(NPAN, -1, depth)
    owner, owner_next = owners[0], owners[1]
    owned = jnp.where(lax.axis_index(COL) == owner, panels[0], panels[1])
    got = spread_pieces(owned)
    right = g2_block.transpose(1, 0, 2).reshape(-1, width)
    got, right = lax.optimization_barrier((got, right))
    both = owner == owner_next
    extra = lax.cond(
        both,
        lambda: lax.optimization_barrier(pick(spread_pieces(panels[1]), owner_next)),
        lambda: jnp.zeros(got.shape[1:], got.dtype),
    )
    halves = gather(jnp.stack([pick(got, owner), jnp.where(both, extra, pick(got, owner_next))]))
    lefts = []
    for index in range(NPAN):
        own, other = halves[0][index], halves[1][index]
        ordered = [jnp.where(core == 0, own, other), jnp.where(core == 0, other, own)]
        lefts.append(turned(jnp.concatenate(ordered, axis=1)))
    sums, sent = reduce_row(lefts, right)
    green, _ = lax.optimization_barrier((green_one, sent))
    src = source(owners, green, rows, width).reshape(NPAN, -1, width)
    rate = jnp.stack([(sums[index] + src[index]).astype(jnp.bfloat16) for index in range(NPAN)])
    return rate.reshape(NPAN, 2, rows, width).transpose(2, 0, 1, 3)


def solution(mesh):
    fine = Mesh(mesh.devices.reshape(tuple(SIZES.values())), tuple(SIZES))
    return jax.shard_map(
        shards,
        mesh=fine,
        in_specs=(P("row", None, COL), P(COL, None, None, None, "row"), P(), P()),
        out_specs=P("row", None, None, COL),
        check_vma=False,
    )
```

profile of v0, /device:TPU:7, one launch (start us, length us, event | category | flops | bytes accessed | tf_op | source)
XLA Modules:
  0.0 126.4 jit_solution(2922022487352157211)
XLA Ops:
  0.0 1.4 %fusion.57 = (s32[1]{0:T(128)}, s32[1]{0:T(128)}) fusion(s32[2]{0:T(128)} %param.8), kind=kLoop, calls=%fused_computation.105 | loop fusion | bytes 16 | tf_op jit(solution)/shard_map/slice | solution.py:90
  3.3 2.1 %slice_select_fusion = bf16[1,1,2,256,512]{4,3,2,1,0:T(8,128)(2,1)} fusion(bf16[1,2,2,256,512]{4,3,2,1,0:T(8,128)(2,1)} %param.7, pred[]{:T(512)S(6)} %eq.78), kind=kLoop, calls=%fused_computation.43 | loop fusion | flops 262144 | bytes 1572865 | tf_op jit(solution)/shard_map/jit(_where)/select_n | solution.py:91
  5.3 15.9 %all-to-all-start.1 = ((bf16[128,8,256]{2,1,0:T(8,128)(2,1)}), bf16[128,8,256]{2,1,0:T(8,128)(2,1)S(1)}, u32[]{:S(2)}, u32[]{:S(2)}) async-start(bf16[128,8,256]{2,1,0:T(8,128)(2,1)} %bitcast.7), calls=%async_computation.1 | async-start | bytes 1048576 | tf_op jit(solution)/shard_map/all_to_all | solution.py:23
  23.7 3.5 %copy.14 = bf16[512,2,1024]{2,0,1:T(8,128)(2,1)} copy(bf16[512,2,1024]{2,1,0:T(2,128)(2,1)} %param.6) | data formatting | bytes 4194304 | tf_op args[0]
  28.5 9.1 %all-to-all-done.1 = bf16[128,8,256]{2,1,0:T(8,128)(2,1)S(1)} async-done(((bf16[128,8,256]{2,1,0:T(8,128)(2,1)}), bf16[128,8,256]{2,1,0:T(8,128)(2,1)S(1)}, u32[]{:S(2)}, u32[]{:S(2)}) %all-to-all-start.1) | async-done | bytes 524320 | tf_op jit(solution)/shard_map/all_to_all | solution.py:23
  37.7 0.8 broadcast_in_dim.2
  38.5 6.8 %all-to-all-start.2 = ((bf16[64,2,8,256]{3,2,1,0:T(8,128)(2,1)}), bf16[64,2,8,256]{3,2,1,0:T(8,128)(2,1)S(1)}, u32[]{:S(2)}, u32[]{:S(2)}) async-start(bf16[64,2,8,256]{3,2,1,0:T(8,128)(2,1)} %broadcast_in_dim.2), calls=%async_computation.2 | async-start | bytes 1048576 | tf_op jit(solution)/shard_map/all_to_all | solution.py:29
  45.4 0.1 sign_compare_fusion.1
  45.5 0.1 ne.109
  45.5 14.8 %all-to-all-done.2 = bf16[64,2,8,256]{3,2,1,0:T(8,128)(2,1)S(1)} async-done(((bf16[64,2,8,256]{3,2,1,0:T(8,128)(2,1)}), bf16[64,2,8,256]{3,2,1,0:T(8,128)(2,1)S(1)}, u32[]{:S(2)}, u32[]{:S(2)}) %all-to-all-start.2) | async-done | bytes 524320 | tf_op jit(solution)/shard_map/all_to_all | solution.py:29
  60.3 4.0 %collective-permute-start = (bf16[64,2,8,256]{3,2,1,0:T(8,128)(2,1)S(1)}, bf16[64,2,8,256]{3,2,1,0:T(8,128)(2,1)S(1)}, u32[]{:S(2)}, u32[]{:S(2)}) collective-permute-start(bf16[64,2,8,256]{3,2,1,0:T(8,128)(2,1)S(1)} %all-to-all-done.2), channel_id=1, source_target_pairs={{0,4},{4,0},{1,5},{5,1},{2,6},{6,2},{3,7},{7,3},{8,12},{12,8},{9,1... | collective-permute-start | bytes 1572872 | tf_op jit(solution)/shard_map/ppermute | solution.py:30
  64.3 0.1 fusion.52
  64.4 0.1 div.24
  64.5 0.1 rem.126
  64.6 1.2 collective-permute-done
  65.9 0.2 fusion.54
  66.1 0.1 pad_maximum_fusion.4
  66.2 0.1 pad_maximum_fusion.1
  66.3 1.3 %copy-done.1 = bf16[512,2,1024]{2,0,1:T(8,128)(2,1)S(1)} copy-done((bf16[512,2,1024]{2,0,1:T(8,128)(2,1)S(1)}, bf16[512,2,1024]{2,0,1:T(8,128)(2,1)}, u32[]{:S(2)}) %copy-start.1) | copy-done | bytes 2097176
  67.7 0.4 convolution_convert_fusion.4
  68.1 0.4 fusion.7
  68.6 0.1 pad_maximum_fusion.2
  68.7 0.1 pad_maximum_fusion
  68.8 0.4 convolution_convert_fusion.5
  69.3 0.4 convolution_convert_fusion.6
  69.7 0.4 convolution_convert_fusion
  70.2 0.4 fusion.8
  70.7 5.0 %collective-permute-start.3 = (bf16[128,1024]{1,0:T(8,128)(2,1)S(1)}, bf16[128,1024]{1,0:T(8,128)(2,1)S(1)}, u32[]{:S(2)}, u32[]{:S(2)}) collective-permute-start(bf16[128,1024]{1,0:T(8,128)(2,1)S(1)} %convolution_convert_fusion.4), channel_id=1, source_target_pairs={{0,3},{1,0},{2,1},{3,2},{4,7},{5,4},{6,5},{7,6},{8,11},{9,8},{10,9... | collective-permute-start | bytes 786440 | tf_op jit(solution)/shard_map/ppermute | solution.py:17
  75.6 1.9 %collective-permute-start.5 = (bf16[128,1024]{1,0:T(8,128)(2,1)S(1)}, bf16[128,1024]{1,0:T(8,128)(2,1)S(1)}, u32[]{:S(2)}, u32[]{:S(2)}) collective-permute-start(bf16[128,1024]{1,0:T(8,128)(2,1)S(1)} %convolution_convert_fusion), channel_id=1, source_target_pairs={{0,1},{1,2},{2,3},{3,0},{4,5},{5,6},{6,7},{7,4},{8,9},{9,10},{10,1... | collective-permute-start | bytes 786440 | tf_op jit(solution)/shard_map/ppermute | solution.py:17
  77.6 0.4 fusion.6
  78.0 5.5 %collective-permute-start.1 = (bf16[128,1024]{1,0:T(8,128)(2,1)S(1)}, bf16[128,1024]{1,0:T(8,128)(2,1)S(1)}, u32[]{:S(2)}, u32[]{:S(2)}) collective-permute-start(bf16[128,1024]{1,0:T(8,128)(2,1)S(1)} %convolution_convert_fusion.6), channel_id=1, source_target_pairs={{0,3},{1,0},{2,1},{3,2},{4,7},{5,4},{6,5},{7,6},{8,11},{9,8},{10,9... | collective-permute-start | bytes 786440 | tf_op jit(solution)/shard_map/ppermute | solution.py:17
  83.5 1.9 %collective-permute-start.2 = (bf16[128,1024]{1,0:T(8,128)(2,1)S(1)}, bf16[128,1024]{1,0:T(8,128)(2,1)S(1)}, u32[]{:S(2)}, u32[]{:S(2)}) collective-permute-start(bf16[128,1024]{1,0:T(8,128)(2,1)S(1)} %convolution_convert_fusion.5), channel_id=1, source_target_pairs={{0,1},{1,2},{2,3},{3,0},{4,5},{5,6},{6,7},{7,4},{8,9},{9,10},{10,1... | collective-permute-start | bytes 786440 | tf_op jit(solution)/shard_map/ppermute | solution.py:17
  85.4 0.4 fusion.9
  85.9 0.4 collective-permute-done.3
  86.3 19.2 %collective-permute-done.2 = bf16[128,1024]{1,0:T(8,128)(2,1)S(1)} collective-permute-done((bf16[128,1024]{1,0:T(8,128)(2,1)S(1)}, bf16[128,1024]{1,0:T(8,128)(2,1)S(1)}, u32[]{:S(2)}, u32[]{:S(2)}) %collective-permute-start.2) | collective-permute-done | bytes 262176 | tf_op jit(solution)/shard_map/ppermute | solution.py:17
  105.6 1.9 %collective-permute-start.6 = (bf16[128,1024]{1,0:T(8,128)(2,1)S(1)}, bf16[128,1024]{1,0:T(8,128)(2,1)S(1)}, u32[]{:S(2)}, u32[]{:S(2)}) collective-permute-start(bf16[128,1024]{1,0:T(8,128)(2,1)S(1)} %add_convert_fusion), channel_id=1, source_target_pairs={{0,3},{1,0},{2,1},{3,2},{4,7},{5,4},{6,5},{7,6},{8,11},{9,8},{10,9... | collective-permute-start | bytes 786440 | tf_op jit(solution)/shard_map/ppermute | solution.py:17
  107.6 4.4 %collective-permute-start.4 = (bf16[128,1024]{1,0:T(8,128)(2,1)S(1)}, bf16[128,1024]{1,0:T(8,128)(2,1)S(1)}, u32[]{:S(2)}, u32[]{:S(2)}) collective-permute-start(bf16[128,1024]{1,0:T(8,128)(2,1)S(1)} %add_convert_fusion.1), channel_id=1, source_target_pairs={{0,1},{1,2},{2,3},{3,0},{4,5},{5,6},{6,7},{7,4},{8,9},{9,10},{10,1... | collective-permute-start | bytes 786440 | tf_op jit(solution)/shard_map/ppermute | solution.py:17
  112.0 1.7 %convolution_bitcast_fusion = f32[2,128,400]{1,2,0:T(8,128)S(1)} fusion(f32[2,400,400]{2,1,0:T(8,128)S(1)} %copy-done, s32[128]{0:T(128)S(1)} %get-tuple-element.44), kind=kOutput, calls=%fused_computation.7 | convolution fusion | flops 491571200 | bytes 1690112 | tf_op jit(solution)/shard_map/qi,cik->cqk/dot_general | solution.py:75
  113.7 1.7 %convolution_bitcast_fusion.1 = f32[2,128,400]{1,2,0:T(8,128)S(1)} fusion(f32[2,400,400]{2,1,0:T(8,128)S(1)} %copy-done, s32[128]{0:T(128)S(1)} %get-tuple-element.43), kind=kOutput, calls=%fused_computation.8 | convolution fusion | flops 491571200 | bytes 1690112 | tf_op jit(solution)/shard_map/qi,cik->cqk/dot_general | solution.py:75
  115.5 1.1 fusion.1
  116.6 1.1 fusion.4
  117.7 0.2 multiply_subtract_fusion
  118.1 6.0 %collective-permute-done.4 = bf16[128,1024]{1,0:T(8,128)(2,1)S(1)} collective-permute-done((bf16[128,1024]{1,0:T(8,128)(2,1)S(1)}, bf16[128,1024]{1,0:T(8,128)(2,1)S(1)}, u32[]{:S(2)}, u32[]{:S(2)}) %collective-permute-start.4) | collective-permute-done | bytes 262176 | tf_op jit(solution)/shard_map/ppermute | solution.py:17
  124.1 0.1 fusion.13
  124.2 0.3 copy.19
  124.5 0.1 fusion.12
  124.7 0.3 copy.20
  125.0 1.5 %maximum_bitcast_fusion.1 = bf16[64,2,2,1024]{3,2,1,0:T(2,128)(2,1)} fusion(bf16[1,2,64,1024]{3,1,0,2:T(2,128)(2,1)S(1)} %copy.20, bf16[1,2,64,1024]{3,1,0,2:T(2,128)(2,1)S(1)} %copy.19), kind=kLoop, calls=%fused_computation.34 | loop fusion | flops 262144 | bytes 1048576 | tf_op jit(solution)/shard_map/transpose | solution.py:111
  (21 shorter events, 0.4 us)
Async XLA Ops:
  0.0 112.0 %copy-start = (f32[2,400,400]{2,1,0:T(8,128)S(1)}, f32[2,400,400]{2,1,0:T(8,128)}, u32[]{:S(2)}) copy-start(f32[2,400,400]{2,1,0:T(8,128)} %param.9) | copy-start | bytes 3840004
  5.3 32.3 %all-to-all-start.1 = ((bf16[128,8,256]{2,1,0:T(8,128)(2,1)}), bf16[128,8,256]{2,1,0:T(8,128)(2,1)S(1)}, u32[]{:S(2)}, u32[]{:S(2)}) async-start(bf16[128,8,256]{2,1,0:T(8,128)(2,1)} %bitcast.7), calls=%async_computation.1 | async-start | bytes 1048576 | tf_op jit(solution)/shard_map/all_to_all | solution.py:23
  23.7 21.6 %copy-start.2 = (s32[2]{0:T(128)S(1)}, s32[2]{0:T(128)}, u32[]{:S(2)}) copy-start(s32[2]{0:T(128)} %param.8) | copy-start | bytes 28
  38.5 21.8 %all-to-all-start.2 = ((bf16[64,2,8,256]{3,2,1,0:T(8,128)(2,1)}), bf16[64,2,8,256]{3,2,1,0:T(8,128)(2,1)S(1)}, u32[]{:S(2)}, u32[]{:S(2)}) async-start(bf16[64,2,8,256]{3,2,1,0:T(8,128)(2,1)} %broadcast_in_dim.2), calls=%async_computation.2 | async-start | bytes 1048576 | tf_op jit(solution)/shard_map/all_to_all | solution.py:29
  60.3 5.5 %collective-permute-start = (bf16[64,2,8,256]{3,2,1,0:T(8,128)(2,1)S(1)}, bf16[64,2,8,256]{3,2,1,0:T(8,128)(2,1)S(1)}, u32[]{:S(2)}, u32[]{:S(2)}) collective-permute-start(bf16[64,2,8,256]{3,2,1,0:T(8,128)(2,1)S(1)} %all-to-all-done.2), channel_id=1, source_target_pairs={{0,4},{4,0},{1,5},{5,1},{2,6},{6,2},{3,7},{7,3},{8,12},{12,8},{9,1... | collective-permute-start | bytes 1572872 | tf_op jit(solution)/shard_map/ppermute | solution.py:30
  66.1 1.6 %copy-start.1 = (bf16[512,2,1024]{2,0,1:T(8,128)(2,1)S(1)}, bf16[512,2,1024]{2,0,1:T(8,128)(2,1)}, u32[]{:S(2)}) copy-start(bf16[512,2,1024]{2,0,1:T(8,128)(2,1)} %copy.14) | copy-start | bytes 6291460
  70.7 15.6 %collective-permute-start.3 = (bf16[128,1024]{1,0:T(8,128)(2,1)S(1)}, bf16[128,1024]{1,0:T(8,128)(2,1)S(1)}, u32[]{:S(2)}, u32[]{:S(2)}) collective-permute-start(bf16[128,1024]{1,0:T(8,128)(2,1)S(1)} %convolution_convert_fusion.4), channel_id=1, source_target_pairs={{0,3},{1,0},{2,1},{3,2},{4,7},{5,4},{6,5},{7,6},{8,11},{9,8},{10,9... | collective-permute-start | bytes 786440 | tf_op jit(solution)/shard_map/ppermute | solution.py:17
  75.6 48.9 %collective-permute-start.5 = (bf16[128,1024]{1,0:T(8,128)(2,1)S(1)}, bf16[128,1024]{1,0:T(8,128)(2,1)S(1)}, u32[]{:S(2)}, u32[]{:S(2)}) collective-permute-start(bf16[128,1024]{1,0:T(8,128)(2,1)S(1)} %convolution_convert_fusion), channel_id=1, source_target_pairs={{0,1},{1,2},{2,3},{3,0},{4,5},{5,6},{6,7},{7,4},{8,9},{9,10},{10,1... | collective-permute-start | bytes 786440 | tf_op jit(solution)/shard_map/ppermute | solution.py:17
  78.0 40.1 %collective-permute-start.1 = (bf16[128,1024]{1,0:T(8,128)(2,1)S(1)}, bf16[128,1024]{1,0:T(8,128)(2,1)S(1)}, u32[]{:S(2)}, u32[]{:S(2)}) collective-permute-start(bf16[128,1024]{1,0:T(8,128)(2,1)S(1)} %convolution_convert_fusion.6), channel_id=1, source_target_pairs={{0,3},{1,0},{2,1},{3,2},{4,7},{5,4},{6,5},{7,6},{8,11},{9,8},{10,9... | collective-permute-start | bytes 786440 | tf_op jit(solution)/shard_map/ppermute | solution.py:17
  83.5 22.0 %collective-permute-start.2 = (bf16[128,1024]{1,0:T(8,128)(2,1)S(1)}, bf16[128,1024]{1,0:T(8,128)(2,1)S(1)}, u32[]{:S(2)}, u32[]{:S(2)}) collective-permute-start(bf16[128,1024]{1,0:T(8,128)(2,1)S(1)} %convolution_convert_fusion.5), channel_id=1, source_target_pairs={{0,1},{1,2},{2,3},{3,0},{4,5},{5,6},{6,7},{7,4},{8,9},{9,10},{10,1... | collective-permute-start | bytes 786440 | tf_op jit(solution)/shard_map/ppermute | solution.py:17
  105.6 19.0 %collective-permute-start.6 = (bf16[128,1024]{1,0:T(8,128)(2,1)S(1)}, bf16[128,1024]{1,0:T(8,128)(2,1)S(1)}, u32[]{:S(2)}, u32[]{:S(2)}) collective-permute-start(bf16[128,1024]{1,0:T(8,128)(2,1)S(1)} %add_convert_fusion), channel_id=1, source_target_pairs={{0,3},{1,0},{2,1},{3,2},{4,7},{5,4},{6,5},{7,6},{8,11},{9,8},{10,9... | collective-permute-start | bytes 786440 | tf_op jit(solution)/shard_map/ppermute | solution.py:17
  107.6 16.5 %collective-permute-start.4 = (bf16[128,1024]{1,0:T(8,128)(2,1)S(1)}, bf16[128,1024]{1,0:T(8,128)(2,1)S(1)}, u32[]{:S(2)}, u32[]{:S(2)}) collective-permute-start(bf16[128,1024]{1,0:T(8,128)(2,1)S(1)} %add_convert_fusion.1), channel_id=1, source_target_pairs={{0,1},{1,2},{2,3},{3,0},{4,5},{5,6},{6,7},{7,4},{8,9},{9,10},{10,1... | collective-permute-start | bytes 786440 | tf_op jit(solution)/shard_map/ppermute | solution.py:17
where the time goes:
time: 127 us; the launch traced here: 126 us
  waiting for transfers between devices  50.8 us (40%)
  starting transfers between devices  47.4 us (37%)
  matrix products  9.18 us (7%)
  local copies, waits for them, and re-layouts  8 us (6%)
  between operations  5.98 us (5%)
  other arithmetic  5.12 us (4%)
    ppermute x6, waiting for transfers between devices, shift(): lax.ppermute(array, 'row', [(index, (index + step) % size) for index in r...  25.7 us
    ppermute x6, starting transfers between devices, shift(): lax.ppermute(array, 'row', [(index, (index + step) % size) for index in r...  20.7 us
    all_to_all x1, starting transfers between devices, spread_pieces(): return lax.all_to_all(pieces, COL, 0, 0, tiled=True)  15.9 us
    all_to_all x1, waiting for transfers between devices, gather(): own = lax.all_to_all(copies, ('y', 'z', 'x'), 0, 0, tiled=True)  14.8 us
    all_to_all x1, waiting for transfers between devices, spread_pieces(): return lax.all_to_all(pieces, COL, 0, 0, tiled=True)  9.14 us
    all_to_all x1, starting transfers between devices, gather(): own = lax.all_to_all(copies, ('y', 'z', 'x'), 0, 0, tiled=True)  6.77 us
    unnamed x7, local copies, waits for them, and re-layouts  4.89 us
    ppermute x1, starting transfers between devices, gather(): other = lax.ppermute(own, 'core', [(0, 1), (1, 0)])  4.01 us
  transfers between devices with their start and end apart: 9, of which 6 were waited for; matrix products, arithmetic and copies ran while one was open for 9% of the time, Pallas kernels for 0%

commit v1 on v0

--- a/solution.py
+++ b/solution.py
@@ -48,8 +48,9 @@
     def with_term(array, index, step):
         return (array.astype(jnp.float32) + term(index, step).astype(jnp.float32)).astype(jnp.bfloat16)
 
-    far = lax.optimization_barrier([shift(term(0, 2), 1), shift(term(1, 2), -1)])
-    straight = [shift(term(0, 3), -1), shift(term(1, 1), 1)]
+    far = [shift(term(0, 2), 1), shift(term(1, 2), -1)]
+    far, sent = lax.optimization_barrier((far, [term(0, 3), term(1, 1)]))
+    straight = [shift(sent[0], -1), shift(sent[1], 1)]
     sent = [with_term(far[0], 0, 1), with_term(far[1], 1, 3)]
     joined = [shift(sent[0], 1), shift(sent[1], -1)]
     own = [term(index, 0) for index in range(NPAN)]

time: 127 us -> 128 us (level)
  the two profiles are of different devices: /device:TPU:7 before, /device:TPU:72 now
where the time goes in v1:
time: 128 us
  waiting for transfers between devices  54.8 us (43%)
  starting transfers between devices  44.7 us (35%)
  matrix products  9.18 us (7%)
  local copies, waits for them, and re-layouts  8.03 us (6%)
  between operations  5.98 us (5%)
  other arithmetic  5.13 us (4%)
    ppermute x6, waiting for transfers between devices, shift(): lax.ppermute(array, 'row', [(index, (index + step) % size) for index in r...  27.2 us
    ppermute x6, starting transfers between devices, shift(): lax.ppermute(array, 'row', [(index, (index + step) % size) for index in r...  22 us
    all_to_all x1, waiting for transfers between devices, gather(): own = lax.all_to_all(copies, ('y', 'z', 'x'), 0, 0, tiled=True)  15.1 us
    all_to_all x1, starting transfers between devices, spread_pieces(): return lax.all_to_all(pieces, COL, 0, 0, tiled=True)  15 us
    all_to_all x1, waiting for transfers between devices, spread_pieces(): return lax.all_to_all(pieces, COL, 0, 0, tiled=True)  10.9 us
    all_to_all x1, starting transfers between devices, gather(): own = lax.all_to_all(copies, ('y', 'z', 'x'), 0, 0, tiled=True)  5.68 us
    unnamed x7, local copies, waits for them, and re-layouts  4.89 us
    dot_general x8, matrix products, term(): jnp.dot(left, right, preferred_element_type=jnp.float32)  3.56 us
  transfers between devices with their start and end apart: 9, of which 6 were waited for; matrix products, arithmetic and copies ran while one was open for 9% of the time, Pallas kernels for 0%

profile of v1, /device:TPU:72, one launch (start us, length us, event | category | flops | bytes accessed | tf_op | source)
XLA Modules:
  0.0 127.8 jit_solution(3717643626502168479)
XLA Ops:
  0.0 1.4 %fusion.57 = (s32[1]{0:T(128)}, s32[1]{0:T(128)}) fusion(s32[2]{0:T(128)} %param.8), kind=kLoop, calls=%fused_computation.105 | loop fusion | bytes 16 | tf_op jit(solution)/shard_map/slice | solution.py:91
  3.3 2.1 %slice_select_fusion = bf16[1,1,2,256,512]{4,3,2,1,0:T(8,128)(2,1)} fusion(bf16[1,2,2,256,512]{4,3,2,1,0:T(8,128)(2,1)} %param.7, pred[]{:T(512)S(6)} %eq.78), kind=kLoop, calls=%fused_computation.43 | loop fusion | flops 262144 | bytes 1572865 | tf_op jit(solution)/shard_map/jit(_where)/select_n | solution.py:92
  5.3 15.0 %all-to-all-start.1 = ((bf16[128,8,256]{2,1,0:T(8,128)(2,1)}), bf16[128,8,256]{2,1,0:T(8,128)(2,1)S(1)}, u32[]{:S(2)}, u32[]{:S(2)}) async-start(bf16[128,8,256]{2,1,0:T(8,128)(2,1)} %bitcast.7), calls=%async_computation.1 | async-start | bytes 1048576 | tf_op jit(solution)/shard_map/all_to_all | solution.py:23
  22.9 3.5 %copy.14 = bf16[512,2,1024]{2,0,1:T(8,128)(2,1)} copy(bf16[512,2,1024]{2,1,0:T(2,128)(2,1)} %param.6) | data formatting | bytes 4194304 | tf_op args[0]
  27.6 10.9 %all-to-all-done.1 = bf16[128,8,256]{2,1,0:T(8,128)(2,1)S(1)} async-done(((bf16[128,8,256]{2,1,0:T(8,128)(2,1)}), bf16[128,8,256]{2,1,0:T(8,128)(2,1)S(1)}, u32[]{:S(2)}, u32[]{:S(2)}) %all-to-all-start.1) | async-done | bytes 524320 | tf_op jit(solution)/shard_map/all_to_all | solution.py:23
  38.5 0.8 broadcast_in_dim.2
  39.4 5.7 %all-to-all-start.2 = ((bf16[64,2,8,256]{3,2,1,0:T(8,128)(2,1)}), bf16[64,2,8,256]{3,2,1,0:T(8,128)(2,1)S(1)}, u32[]{:S(2)}, u32[]{:S(2)}) async-start(bf16[64,2,8,256]{3,2,1,0:T(8,128)(2,1)} %broadcast_in_dim.2), calls=%async_computation.2 | async-start | bytes 1048576 | tf_op jit(solution)/shard_map/all_to_all | solution.py:29
  45.2 0.1 ne.109
  45.3 15.1 %all-to-all-done.2 = bf16[64,2,8,256]{3,2,1,0:T(8,128)(2,1)S(1)} async-done(((bf16[64,2,8,256]{3,2,1,0:T(8,128)(2,1)}), bf16[64,2,8,256]{3,2,1,0:T(8,128)(2,1)S(1)}, u32[]{:S(2)}, u32[]{:S(2)}) %all-to-all-start.2) | async-done | bytes 524320 | tf_op jit(solution)/shard_map/all_to_all | solution.py:29
  60.4 1.9 %collective-permute-start = (bf16[64,2,8,256]{3,2,1,0:T(8,128)(2,1)S(1)}, bf16[64,2,8,256]{3,2,1,0:T(8,128)(2,1)S(1)}, u32[]{:S(2)}, u32[]{:S(2)}) collective-permute-start(bf16[64,2,8,256]{3,2,1,0:T(8,128)(2,1)S(1)} %all-to-all-done.2), channel_id=1, source_target_pairs={{0,4},{4,0},{1,5},{5,1},{2,6},{6,2},{3,7},{7,3},{8,12},{12,8},{9,1... | collective-permute-start | bytes 1572872 | tf_op jit(solution)/shard_map/ppermute | solution.py:30
  62.3 0.1 fusion.52
  62.4 0.1 div.24
  62.5 0.1 rem.126
  62.6 1.6 %collective-permute-done = bf16[64,2,8,256]{3,2,1,0:T(8,128)(2,1)S(1)} collective-permute-done((bf16[64,2,8,256]{3,2,1,0:T(8,128)(2,1)S(1)}, bf16[64,2,8,256]{3,2,1,0:T(8,128)(2,1)S(1)}, u32[]{:S(2)}, u32[]{:S(2)}) %collective-permute-start) | collective-permute-done | bytes 524320 | tf_op jit(solution)/shard_map/ppermute | solution.py:30
  64.3 0.2 fusion.54
  64.5 0.1 pad_maximum_fusion.4
  64.6 0.1 pad_maximum_fusion.1
  64.7 1.3 %copy-done.1 = bf16[512,2,1024]{2,0,1:T(8,128)(2,1)S(1)} copy-done((bf16[512,2,1024]{2,0,1:T(8,128)(2,1)S(1)}, bf16[512,2,1024]{2,0,1:T(8,128)(2,1)}, u32[]{:S(2)}) %copy-start.1) | copy-done | bytes 2097176
  66.1 0.4 convolution_convert_fusion.3
  66.5 0.4 convolution_convert_fusion.5
  67.0 0.1 pad_maximum_fusion.2
  67.1 0.1 pad_maximum_fusion
  67.2 0.4 convolution_convert_fusion.6
  67.7 0.4 fusion.8
  68.1 0.4 fusion.6
  68.6 0.4 fusion.9
  69.0 5.3 %collective-permute-start.2 = (bf16[128,1024]{1,0:T(8,128)(2,1)S(1)}, bf16[128,1024]{1,0:T(8,128)(2,1)S(1)}, u32[]{:S(2)}, u32[]{:S(2)}) collective-permute-start(bf16[128,1024]{1,0:T(8,128)(2,1)S(1)} %convolution_convert_fusion.5), channel_id=1, source_target_pairs={{0,3},{1,0},{2,1},{3,2},{4,7},{5,4},{6,5},{7,6},{8,11},{9,8},{10,9... | collective-permute-start | bytes 786440 | tf_op jit(solution)/shard_map/ppermute | solution.py:17
  74.3 0.4 fusion.7
  74.8 1.9 %collective-permute-start.1 = (bf16[128,1024]{1,0:T(8,128)(2,1)S(1)}, bf16[128,1024]{1,0:T(8,128)(2,1)S(1)}, u32[]{:S(2)}, u32[]{:S(2)}) collective-permute-start(bf16[128,1024]{1,0:T(8,128)(2,1)S(1)} %convolution_convert_fusion.6), channel_id=1, source_target_pairs={{0,1},{1,2},{2,3},{3,0},{4,5},{5,6},{6,7},{7,4},{8,9},{9,10},{10,1... | collective-permute-start | bytes 786440 | tf_op jit(solution)/shard_map/ppermute | solution.py:17
  76.7 0.4 convolution_convert_fusion.4
  77.1 8.5 %collective-permute-done.2 = bf16[128,1024]{1,0:T(8,128)(2,1)S(1)} collective-permute-done((bf16[128,1024]{1,0:T(8,128)(2,1)S(1)}, bf16[128,1024]{1,0:T(8,128)(2,1)S(1)}, u32[]{:S(2)}, u32[]{:S(2)}) %collective-permute-start.2) | collective-permute-done | bytes 262176 | tf_op jit(solution)/shard_map/ppermute | solution.py:17
  85.6 6.8 %collective-permute-done.1 = bf16[128,1024]{1,0:T(8,128)(2,1)S(1)} collective-permute-done((bf16[128,1024]{1,0:T(8,128)(2,1)S(1)}, bf16[128,1024]{1,0:T(8,128)(2,1)S(1)}, u32[]{:S(2)}, u32[]{:S(2)}) %collective-permute-start.1) | collective-permute-done | bytes 262176 | tf_op jit(solution)/shard_map/ppermute | solution.py:17
  92.4 2.9 %collective-permute-start.3 = (bf16[128,1024]{1,0:T(8,128)(2,1)S(1)}, bf16[128,1024]{1,0:T(8,128)(2,1)S(1)}, u32[]{:S(2)}, u32[]{:S(2)}) collective-permute-start(bf16[128,1024]{1,0:T(8,128)(2,1)S(1)} %convolution_convert_fusion.4), channel_id=1, source_target_pairs={{0,3},{1,0},{2,1},{3,2},{4,7},{5,4},{6,5},{7,6},{8,11},{9,8},{10,9... | collective-permute-start | bytes 786440 | tf_op jit(solution)/shard_map/ppermute | solution.py:17
  95.4 4.3 %collective-permute-start.6 = (bf16[128,1024]{1,0:T(8,128)(2,1)S(1)}, bf16[128,1024]{1,0:T(8,128)(2,1)S(1)}, u32[]{:S(2)}, u32[]{:S(2)}) collective-permute-start(bf16[128,1024]{1,0:T(8,128)(2,1)S(1)} %add_convert_fusion), channel_id=1, source_target_pairs={{0,3},{1,0},{2,1},{3,2},{4,7},{5,4},{6,5},{7,6},{8,11},{9,8},{10,9... | collective-permute-start | bytes 786440 | tf_op jit(solution)/shard_map/ppermute | solution.py:17
  99.7 2.5 %collective-permute-start.5 = (bf16[128,1024]{1,0:T(8,128)(2,1)S(1)}, bf16[128,1024]{1,0:T(8,128)(2,1)S(1)}, u32[]{:S(2)}, u32[]{:S(2)}) collective-permute-start(bf16[128,1024]{1,0:T(8,128)(2,1)S(1)} %convolution_convert_fusion.3), channel_id=1, source_target_pairs={{0,1},{1,2},{2,3},{3,0},{4,5},{5,6},{6,7},{7,4},{8,9},{9,10},{10,1... | collective-permute-start | bytes 786440 | tf_op jit(solution)/shard_map/ppermute | solution.py:17
  102.2 5.2 %collective-permute-start.4 = (bf16[128,1024]{1,0:T(8,128)(2,1)S(1)}, bf16[128,1024]{1,0:T(8,128)(2,1)S(1)}, u32[]{:S(2)}, u32[]{:S(2)}) collective-permute-start(bf16[128,1024]{1,0:T(8,128)(2,1)S(1)} %add_convert_fusion.1), channel_id=1, source_target_pairs={{0,1},{1,2},{2,3},{3,0},{4,5},{5,6},{6,7},{7,4},{8,9},{9,10},{10,1... | collective-permute-start | bytes 786440 | tf_op jit(solution)/shard_map/ppermute | solution.py:17
  107.5 1.7 %convolution_bitcast_fusion = f32[2,128,400]{1,2,0:T(8,128)S(1)} fusion(f32[2,400,400]{2,1,0:T(8,128)S(1)} %copy-done, s32[128]{0:T(128)S(1)} %get-tuple-element.48), kind=kOutput, calls=%fused_computation.7 | convolution fusion | flops 491571200 | bytes 1690112 | tf_op jit(solution)/shard_map/qi,cik->cqk/dot_general | solution.py:76
  109.2 1.7 %convolution_bitcast_fusion.1 = f32[2,128,400]{1,2,0:T(8,128)S(1)} fusion(f32[2,400,400]{2,1,0:T(8,128)S(1)} %copy-done, s32[128]{0:T(128)S(1)} %get-tuple-element.47), kind=kOutput, calls=%fused_computation.8 | convolution fusion | flops 491571200 | bytes 1690112 | tf_op jit(solution)/shard_map/qi,cik->cqk/dot_general | solution.py:76
  110.9 1.1 fusion.1
  112.0 1.1 fusion.4
  113.1 0.2 multiply_subtract_fusion
  113.4 0.1 fusion.56
  113.6 11.9 %collective-permute-done.4 = bf16[128,1024]{1,0:T(8,128)(2,1)S(1)} collective-permute-done((bf16[128,1024]{1,0:T(8,128)(2,1)S(1)}, bf16[128,1024]{1,0:T(8,128)(2,1)S(1)}, u32[]{:S(2)}, u32[]{:S(2)}) %collective-permute-start.4) | collective-permute-done | bytes 262176 | tf_op jit(solution)/shard_map/ppermute | solution.py:17
  125.5 0.1 fusion.13
  125.6 0.3 copy.19
  125.9 0.1 fusion.12
  126.1 0.3 copy.20
  126.3 1.5 %maximum_bitcast_fusion.1 = bf16[64,2,2,1024]{3,2,1,0:T(2,128)(2,1)} fusion(bf16[1,2,64,1024]{3,1,0,2:T(2,128)(2,1)S(1)} %copy.20, bf16[1,2,64,1024]{3,1,0,2:T(2,128)(2,1)S(1)} %copy.19), kind=kLoop, calls=%fused_computation.34 | loop fusion | flops 262144 | bytes 1048576 | tf_op jit(solution)/shard_map/transpose | solution.py:112
  (21 shorter events, 0.4 us)
Async XLA Ops:
  0.0 107.5 %copy-start = (f32[2,400,400]{2,1,0:T(8,128)S(1)}, f32[2,400,400]{2,1,0:T(8,128)}, u32[]{:S(2)}) copy-start(f32[2,400,400]{2,1,0:T(8,128)} %param.9) | copy-start | bytes 3840004
  5.3 33.2 %all-to-all-start.1 = ((bf16[128,8,256]{2,1,0:T(8,128)(2,1)}), bf16[128,8,256]{2,1,0:T(8,128)(2,1)S(1)}, u32[]{:S(2)}, u32[]{:S(2)}) async-start(bf16[128,8,256]{2,1,0:T(8,128)(2,1)} %bitcast.7), calls=%async_computation.1 | async-start | bytes 1048576 | tf_op jit(solution)/shard_map/all_to_all | solution.py:23
  22.9 22.3 %copy-start.2 = (s32[2]{0:T(128)S(1)}, s32[2]{0:T(128)}, u32[]{:S(2)}) copy-start(s32[2]{0:T(128)} %param.8) | copy-start | bytes 28
  39.4 21.0 %all-to-all-start.2 = ((bf16[64,2,8,256]{3,2,1,0:T(8,128)(2,1)}), bf16[64,2,8,256]{3,2,1,0:T(8,128)(2,1)S(1)}, u32[]{:S(2)}, u32[]{:S(2)}) async-start(bf16[64,2,8,256]{3,2,1,0:T(8,128)(2,1)} %broadcast_in_dim.2), calls=%async_computation.2 | async-start | bytes 1048576 | tf_op jit(solution)/shard_map/all_to_all | solution.py:29
  60.4 3.8 %collective-permute-start = (bf16[64,2,8,256]{3,2,1,0:T(8,128)(2,1)S(1)}, bf16[64,2,8,256]{3,2,1,0:T(8,128)(2,1)S(1)}, u32[]{:S(2)}, u32[]{:S(2)}) collective-permute-start(bf16[64,2,8,256]{3,2,1,0:T(8,128)(2,1)S(1)} %all-to-all-done.2), channel_id=1, source_target_pairs={{0,4},{4,0},{1,5},{5,1},{2,6},{6,2},{3,7},{7,3},{8,12},{12,8},{9,1... | collective-permute-start | bytes 1572872 | tf_op jit(solution)/shard_map/ppermute | solution.py:30
  64.5 1.6 %copy-start.1 = (bf16[512,2,1024]{2,0,1:T(8,128)(2,1)S(1)}, bf16[512,2,1024]{2,0,1:T(8,128)(2,1)}, u32[]{:S(2)}) copy-start(bf16[512,2,1024]{2,0,1:T(8,128)(2,1)} %copy.14) | copy-start | bytes 6291460
  69.0 16.6 %collective-permute-start.2 = (bf16[128,1024]{1,0:T(8,128)(2,1)S(1)}, bf16[128,1024]{1,0:T(8,128)(2,1)S(1)}, u32[]{:S(2)}, u32[]{:S(2)}) collective-permute-start(bf16[128,1024]{1,0:T(8,128)(2,1)S(1)} %convolution_convert_fusion.5), channel_id=1, source_target_pairs={{0,3},{1,0},{2,1},{3,2},{4,7},{5,4},{6,5},{7,6},{8,11},{9,8},{10,9... | collective-permute-start | bytes 786440 | tf_op jit(solution)/shard_map/ppermute | solution.py:17
  74.8 17.7 %collective-permute-start.1 = (bf16[128,1024]{1,0:T(8,128)(2,1)S(1)}, bf16[128,1024]{1,0:T(8,128)(2,1)S(1)}, u32[]{:S(2)}, u32[]{:S(2)}) collective-permute-start(bf16[128,1024]{1,0:T(8,128)(2,1)S(1)} %convolution_convert_fusion.6), channel_id=1, source_target_pairs={{0,1},{1,2},{2,3},{3,0},{4,5},{5,6},{6,7},{7,4},{8,9},{9,10},{10,1... | collective-permute-start | bytes 786440 | tf_op jit(solution)/shard_map/ppermute | solution.py:17
  92.4 21.1 %collective-permute-start.3 = (bf16[128,1024]{1,0:T(8,128)(2,1)S(1)}, bf16[128,1024]{1,0:T(8,128)(2,1)S(1)}, u32[]{:S(2)}, u32[]{:S(2)}) collective-permute-start(bf16[128,1024]{1,0:T(8,128)(2,1)S(1)} %convolution_convert_fusion.4), channel_id=1, source_target_pairs={{0,3},{1,0},{2,1},{3,2},{4,7},{5,4},{6,5},{7,6},{8,11},{9,8},{10,9... | collective-permute-start | bytes 786440 | tf_op jit(solution)/shard_map/ppermute | solution.py:17
  95.4 30.5 %collective-permute-start.6 = (bf16[128,1024]{1,0:T(8,128)(2,1)S(1)}, bf16[128,1024]{1,0:T(8,128)(2,1)S(1)}, u32[]{:S(2)}, u32[]{:S(2)}) collective-permute-start(bf16[128,1024]{1,0:T(8,128)(2,1)S(1)} %add_convert_fusion), channel_id=1, source_target_pairs={{0,3},{1,0},{2,1},{3,2},{4,7},{5,4},{6,5},{7,6},{8,11},{9,8},{10,9... | collective-permute-start | bytes 786440 | tf_op jit(solution)/shard_map/ppermute | solution.py:17
  99.7 26.2 %collective-permute-start.5 = (bf16[128,1024]{1,0:T(8,128)(2,1)S(1)}, bf16[128,1024]{1,0:T(8,128)(2,1)S(1)}, u32[]{:S(2)}, u32[]{:S(2)}) collective-permute-start(bf16[128,1024]{1,0:T(8,128)(2,1)S(1)} %convolution_convert_fusion.3), channel_id=1, source_target_pairs={{0,1},{1,2},{2,3},{3,0},{4,5},{5,6},{6,7},{7,4},{8,9},{9,10},{10,1... | collective-permute-start | bytes 786440 | tf_op jit(solution)/shard_map/ppermute | solution.py:17
  102.2 23.3 %collective-permute-start.4 = (bf16[128,1024]{1,0:T(8,128)(2,1)S(1)}, bf16[128,1024]{1,0:T(8,128)(2,1)S(1)}, u32[]{:S(2)}, u32[]{:S(2)}) collective-permute-start(bf16[128,1024]{1,0:T(8,128)(2,1)S(1)} %add_convert_fusion.1), channel_id=1, source_target_pairs={{0,1},{1,2},{2,3},{3,0},{4,5},{5,6},{6,7},{7,4},{8,9},{9,10},{10,1... | collective-permute-start | bytes 786440 | tf_op jit(solution)/shard_map/ppermute | solution.py:17

commit v2 on v1

--- a/solution.py
+++ b/solution.py
@@ -49,15 +49,14 @@
         return (array.astype(jnp.float32) + term(index, step).astype(jnp.float32)).astype(jnp.bfloat16)
 
     far = [shift(term(0, 2), 1), shift(term(1, 2), -1)]
-    far, sent = lax.optimization_barrier((far, [term(0, 3), term(1, 1)]))
-    straight = [shift(sent[0], -1), shift(sent[1], 1)]
-    sent = [with_term(far[0], 0, 1), with_term(far[1], 1, 3)]
-    joined = [shift(sent[0], 1), shift(sent[1], -1)]
-    own = [term(index, 0) for index in range(NPAN)]
-    sums = [
-        own[index].astype(jnp.float32) + straight[index].astype(jnp.float32) + joined[index].astype(jnp.float32)
-        for index in range(NPAN)
+    sent = [
+        jnp.concatenate([with_term(far[0], 0, 1), term(1, 1)]),
+        jnp.concatenate([term(0, 3), with_term(far[1], 1, 3)]),
     ]
+    sent, lefts = lax.optimization_barrier((sent, lefts))
+    from_left = shift(sent[0], 1).reshape(NPAN, -1, right.shape[1]).astype(jnp.float32)
+    from_right = shift(sent[1], -1).reshape(NPAN, -1, right.shape[1]).astype(jnp.float32)
+    sums = [term(index, 0).astype(jnp.float32) + from_left[index] + from_right[index] for index in range(NPAN)]
     return sums, sent
 
 

time: 128 us -> 124 us (0.969)
  the two profiles are of different devices: /device:TPU:72 before, /device:TPU:112 now
where the time goes in v2:
time: 124 us; the launch traced here: 123 us
  waiting for transfers between devices  58 us (47%)
  starting transfers between devices  37 us (30%)
  matrix products  9.24 us (7%)
  local copies, waits for them, and re-layouts  7.99 us (6%)
  between operations  6.09 us (5%)
  other arithmetic  5.05 us (4%)
    ppermute x4, waiting for transfers between devices, shift(): lax.ppermute(array, 'row', [(index, (index + step) % size) for index in r...  29.2 us
    all_to_all x1, waiting for transfers between devices, gather(): own = lax.all_to_all(copies, ('y', 'z', 'x'), 0, 0, tiled=True)  16 us
    ppermute x4, starting transfers between devices, shift(): lax.ppermute(array, 'row', [(index, (index + step) % size) for index in r...  15.6 us
    all_to_all x1, starting transfers between devices, spread_pieces(): return lax.all_to_all(pieces, COL, 0, 0, tiled=True)  13.9 us
    all_to_all x1, waiting for transfers between devices, spread_pieces(): return lax.all_to_all(pieces, COL, 0, 0, tiled=True)  11.1 us
    all_to_all x1, starting transfers between devices, gather(): own = lax.all_to_all(copies, ('y', 'z', 'x'), 0, 0, tiled=True)  5.55 us
    unnamed x7, local copies, waits for them, and re-layouts  4.89 us
    dot_general x8, matrix products, term(): jnp.dot(left, right, preferred_element_type=jnp.float32)  3.62 us
  transfers between devices with their start and end apart: 7, of which 7 were waited for; matrix products, arithmetic and copies ran while one was open for 9% of the time, Pallas kernels for 0%

profile of v2, /device:TPU:112, one launch (start us, length us, event | category | flops | bytes accessed | tf_op | source)
XLA Modules:
  0.0 123.4 jit_solution(16383231534436798626)
XLA Ops:
  0.0 1.4 %fusion.67 = (s32[1]{0:T(128)}, s32[1]{0:T(128)}) fusion(s32[2]{0:T(128)} %param.8), kind=kLoop, calls=%fused_computation.111 | loop fusion | bytes 16 | tf_op jit(solution)/shard_map/slice | solution.py:90
  3.3 2.1 %slice_select_fusion = bf16[1,1,2,256,512]{4,3,2,1,0:T(8,128)(2,1)} fusion(bf16[1,2,2,256,512]{4,3,2,1,0:T(8,128)(2,1)} %param.7, pred[]{:T(512)S(6)} %eq.78), kind=kLoop, calls=%fused_computation.49 | loop fusion | flops 262144 | bytes 1572865 | tf_op jit(solution)/shard_map/jit(_where)/select_n | solution.py:91
  5.4 13.9 %all-to-all-start.1 = ((bf16[128,8,256]{2,1,0:T(8,128)(2,1)}), bf16[128,8,256]{2,1,0:T(8,128)(2,1)S(1)}, u32[]{:S(2)}, u32[]{:S(2)}) async-start(bf16[128,8,256]{2,1,0:T(8,128)(2,1)} %bitcast.7), calls=%async_computation.1 | async-start | bytes 1048576 | tf_op jit(solution)/shard_map/all_to_all | solution.py:23
  21.8 3.5 %copy.14 = bf16[512,2,1024]{2,0,1:T(8,128)(2,1)} copy(bf16[512,2,1024]{2,1,0:T(2,128)(2,1)} %param.6) | data formatting | bytes 4194304 | tf_op args[0]
  26.6 11.1 %all-to-all-done.1 = bf16[128,8,256]{2,1,0:T(8,128)(2,1)S(1)} async-done(((bf16[128,8,256]{2,1,0:T(8,128)(2,1)}), bf16[128,8,256]{2,1,0:T(8,128)(2,1)S(1)}, u32[]{:S(2)}, u32[]{:S(2)}) %all-to-all-start.1) | async-done | bytes 524320 | tf_op jit(solution)/shard_map/all_to_all | solution.py:23
  37.8 0.8 broadcast_in_dim.2
  38.6 5.6 %all-to-all-start.2 = ((bf16[64,2,8,256]{3,2,1,0:T(8,128)(2,1)}), bf16[64,2,8,256]{3,2,1,0:T(8,128)(2,1)S(1)}, u32[]{:S(2)}, u32[]{:S(2)}) async-start(bf16[64,2,8,256]{3,2,1,0:T(8,128)(2,1)} %broadcast_in_dim.2), calls=%async_computation.2 | async-start | bytes 1048576 | tf_op jit(solution)/shard_map/all_to_all | solution.py:29
  44.2 0.1 fusion.62
  44.3 0.1 div.24
  44.4 0.1 rem.126
  44.5 16.0 %all-to-all-done.2 = bf16[64,2,8,256]{3,2,1,0:T(8,128)(2,1)S(1)} async-done(((bf16[64,2,8,256]{3,2,1,0:T(8,128)(2,1)}), bf16[64,2,8,256]{3,2,1,0:T(8,128)(2,1)S(1)}, u32[]{:S(2)}, u32[]{:S(2)}) %all-to-all-start.2) | async-done | bytes 524320 | tf_op jit(solution)/shard_map/all_to_all | solution.py:29
  60.5 1.9 %collective-permute-start = (bf16[64,2,8,256]{3,2,1,0:T(8,128)(2,1)S(1)}, bf16[64,2,8,256]{3,2,1,0:T(8,128)(2,1)S(1)}, u32[]{:S(2)}, u32[]{:S(2)}) collective-permute-start(bf16[64,2,8,256]{3,2,1,0:T(8,128)(2,1)S(1)} %all-to-all-done.2), channel_id=1, source_target_pairs={{0,4},{4,0},{1,5},{5,1},{2,6},{6,2},{3,7},{7,3},{8,12},{12,8},{9,1... | collective-permute-start | bytes 1572872 | tf_op jit(solution)/shard_map/ppermute | solution.py:30
  62.4 0.1 sign_compare_fusion.1
  62.5 0.1 ne.109
  62.6 1.7 %collective-permute-done = bf16[64,2,8,256]{3,2,1,0:T(8,128)(2,1)S(1)} collective-permute-done((bf16[64,2,8,256]{3,2,1,0:T(8,128)(2,1)S(1)}, bf16[64,2,8,256]{3,2,1,0:T(8,128)(2,1)S(1)}, u32[]{:S(2)}, u32[]{:S(2)}) %collective-permute-start) | collective-permute-done | bytes 524320 | tf_op jit(solution)/shard_map/ppermute | solution.py:30
  64.3 0.1 select_bitcast_fusion.2
  64.4 0.2 fusion.64
  64.6 0.1 pad_maximum_fusion.2
  64.7 0.1 pad_maximum_fusion
  64.8 1.3 %copy-done.1 = bf16[512,2,1024]{2,0,1:T(8,128)(2,1)S(1)} copy-done((bf16[512,2,1024]{2,0,1:T(8,128)(2,1)S(1)}, bf16[512,2,1024]{2,0,1:T(8,128)(2,1)}, u32[]{:S(2)}) %copy-start.1) | copy-done | bytes 2097176
  66.2 0.4 convolution_convert_fusion.4
  66.6 0.4 convolution_convert_fusion.7
  67.1 0.1 pad_maximum_fusion.4
  67.2 0.1 pad_maximum_fusion.1
  67.3 0.4 convolution_convert_fusion.3
  67.8 4.0 %collective-permute-start.2 = (bf16[128,1024]{1,0:T(8,128)(2,1)S(1)}, bf16[128,1024]{1,0:T(8,128)(2,1)S(1)}, u32[]{:S(2)}, u32[]{:S(2)}) collective-permute-start(bf16[128,1024]{1,0:T(8,128)(2,1)S(1)} %convolution_convert_fusion.3), channel_id=1, source_target_pairs={{0,3},{1,0},{2,1},{3,2},{4,7},{5,4},{6,5},{7,6},{8,11},{9,8},{10,9... | collective-permute-start | bytes 786440 | tf_op jit(solution)/shard_map/ppermute | solution.py:17
  71.8 3.9 %collective-permute-start.1 = (bf16[128,1024]{1,0:T(8,128)(2,1)S(1)}, bf16[128,1024]{1,0:T(8,128)(2,1)S(1)}, u32[]{:S(2)}, u32[]{:S(2)}) collective-permute-start(bf16[128,1024]{1,0:T(8,128)(2,1)S(1)} %convolution_convert_fusion.7), channel_id=1, source_target_pairs={{0,1},{1,2},{2,3},{3,0},{4,5},{5,6},{6,7},{7,4},{8,9},{9,10},{10,1... | collective-permute-start | bytes 786440 | tf_op jit(solution)/shard_map/ppermute | solution.py:17
  75.7 0.4 convolution_convert_fusion.5
  76.2 8.7 %collective-permute-done.2 = bf16[128,1024]{1,0:T(8,128)(2,1)S(1)} collective-permute-done((bf16[128,1024]{1,0:T(8,128)(2,1)S(1)}, bf16[128,1024]{1,0:T(8,128)(2,1)S(1)}, u32[]{:S(2)}, u32[]{:S(2)}) %collective-permute-start.2) | collective-permute-done | bytes 262176 | tf_op jit(solution)/shard_map/ppermute | solution.py:17
  84.9 0.4 add_convert_fusion
  85.4 0.8 collective-permute-done.1
  86.2 0.4 add_convert_fusion.1
  86.7 5.5 %collective-permute-start.3 = (bf16[256,1024]{1,0:T(8,128)(2,1)S(1)}, bf16[256,1024]{1,0:T(8,128)(2,1)S(1)}, u32[]{:S(2)}, u32[]{:S(2)}) collective-permute-start(bf16[256,1024]{1,0:T(8,128)(2,1)S(1)} %pad_maximum_fusion.6), channel_id=1, source_target_pairs={{0,1},{1,2},{2,3},{3,0},{4,5},{5,6},{6,7},{7,4},{8,9},{9,10},{10,1... | collective-permute-start | bytes 1572872 | tf_op jit(solution)/shard_map/ppermute | solution.py:17
  92.3 2.1 %collective-permute-start.4 = (bf16[256,1024]{1,0:T(8,128)(2,1)S(1)}, bf16[256,1024]{1,0:T(8,128)(2,1)S(1)}, u32[]{:S(2)}, u32[]{:S(2)}) collective-permute-start(bf16[256,1024]{1,0:T(8,128)(2,1)S(1)} %pad_maximum_fusion.7), channel_id=1, source_target_pairs={{0,3},{1,0},{2,1},{3,2},{4,7},{5,4},{6,5},{7,6},{8,11},{9,8},{10,9... | collective-permute-start | bytes 1572872 | tf_op jit(solution)/shard_map/ppermute | solution.py:17
  94.4 1.7 %convolution_bitcast_fusion.1 = f32[2,128,400]{1,2,0:T(8,128)S(1)} fusion(f32[2,400,400]{2,1,0:T(8,128)S(1)} %copy-done, s32[128]{0:T(128)S(1)} %get-tuple-element.47), kind=kOutput, calls=%fused_computation.8 | convolution fusion | flops 491571200 | bytes 1690112 | tf_op jit(solution)/shard_map/qi,cik->cqk/dot_general | solution.py:75
  96.1 1.7 %convolution_bitcast_fusion = f32[2,128,400]{1,2,0:T(8,128)S(1)} fusion(f32[2,400,400]{2,1,0:T(8,128)S(1)} %copy-done, s32[128]{0:T(128)S(1)} %get-tuple-element.48), kind=kOutput, calls=%fused_computation.7 | convolution fusion | flops 491571200 | bytes 1690112 | tf_op jit(solution)/shard_map/qi,cik->cqk/dot_general | solution.py:75
  97.9 1.1 fusion.1
  99.0 1.1 fusion.4
  100.1 0.2 multiply_subtract_fusion
  100.5 13.8 %collective-permute-done.3 = bf16[256,1024]{1,0:T(8,128)(2,1)S(1)} collective-permute-done((bf16[256,1024]{1,0:T(8,128)(2,1)S(1)}, bf16[256,1024]{1,0:T(8,128)(2,1)S(1)}, u32[]{:S(2)}, u32[]{:S(2)}) %collective-permute-start.3) | collective-permute-done | bytes 524320 | tf_op jit(solution)/shard_map/ppermute | solution.py:17
  114.3 0.1 convert_element_type.84
  114.4 5.9 %collective-permute-done.4 = bf16[256,1024]{1,0:T(8,128)(2,1)S(1)} collective-permute-done((bf16[256,1024]{1,0:T(8,128)(2,1)S(1)}, bf16[256,1024]{1,0:T(8,128)(2,1)S(1)}, u32[]{:S(2)}, u32[]{:S(2)}) %collective-permute-start.4) | collective-permute-done | bytes 524320 | tf_op jit(solution)/shard_map/ppermute | solution.py:17
  120.3 0.1 convert_element_type.85
  120.4 0.5 fusion.15
  120.8 0.3 copy.19
  121.1 0.5 fusion.13
  121.6 0.3 copy.20
  121.9 1.5 %maximum_bitcast_fusion.1 = bf16[64,2,2,1024]{3,2,1,0:T(2,128)(2,1)} fusion(bf16[1,2,64,1024]{3,1,0,2:T(2,128)(2,1)S(1)} %copy.20, bf16[1,2,64,1024]{3,1,0,2:T(2,128)(2,1)S(1)} %copy.19), kind=kLoop, calls=%fused_computation.44 | loop fusion | flops 262144 | bytes 1048576 | tf_op jit(solution)/shard_map/transpose | solution.py:111
  (17 shorter events, 0.3 us)
Async XLA Ops:
  0.0 94.4 %copy-start = (f32[2,400,400]{2,1,0:T(8,128)S(1)}, f32[2,400,400]{2,1,0:T(8,128)}, u32[]{:S(2)}) copy-start(f32[2,400,400]{2,1,0:T(8,128)} %param.9) | copy-start | bytes 3840004
  5.4 32.4 %all-to-all-start.1 = ((bf16[128,8,256]{2,1,0:T(8,128)(2,1)}), bf16[128,8,256]{2,1,0:T(8,128)(2,1)S(1)}, u32[]{:S(2)}, u32[]{:S(2)}) async-start(bf16[128,8,256]{2,1,0:T(8,128)(2,1)} %bitcast.7), calls=%async_computation.1 | async-start | bytes 1048576 | tf_op jit(solution)/shard_map/all_to_all | solution.py:23
  21.8 22.4 %copy-start.2 = (s32[2]{0:T(128)S(1)}, s32[2]{0:T(128)}, u32[]{:S(2)}) copy-start(s32[2]{0:T(128)} %param.8) | copy-start | bytes 28
  38.6 21.9 %all-to-all-start.2 = ((bf16[64,2,8,256]{3,2,1,0:T(8,128)(2,1)}), bf16[64,2,8,256]{3,2,1,0:T(8,128)(2,1)S(1)}, u32[]{:S(2)}, u32[]{:S(2)}) async-start(bf16[64,2,8,256]{3,2,1,0:T(8,128)(2,1)} %broadcast_in_dim.2), calls=%async_computation.2 | async-start | bytes 1048576 | tf_op jit(solution)/shard_map/all_to_all | solution.py:29
  60.5 3.8 %collective-permute-start = (bf16[64,2,8,256]{3,2,1,0:T(8,128)(2,1)S(1)}, bf16[64,2,8,256]{3,2,1,0:T(8,128)(2,1)S(1)}, u32[]{:S(2)}, u32[]{:S(2)}) collective-permute-start(bf16[64,2,8,256]{3,2,1,0:T(8,128)(2,1)S(1)} %all-to-all-done.2), channel_id=1, source_target_pairs={{0,4},{4,0},{1,5},{5,1},{2,6},{6,2},{3,7},{7,3},{8,12},{12,8},{9,1... | collective-permute-start | bytes 1572872 | tf_op jit(solution)/shard_map/ppermute | solution.py:30
  64.6 1.6 %copy-start.1 = (bf16[512,2,1024]{2,0,1:T(8,128)(2,1)S(1)}, bf16[512,2,1024]{2,0,1:T(8,128)(2,1)}, u32[]{:S(2)}) copy-start(bf16[512,2,1024]{2,0,1:T(8,128)(2,1)} %copy.14) | copy-start | bytes 6291460
  67.8 17.1 %collective-permute-start.2 = (bf16[128,1024]{1,0:T(8,128)(2,1)S(1)}, bf16[128,1024]{1,0:T(8,128)(2,1)S(1)}, u32[]{:S(2)}, u32[]{:S(2)}) collective-permute-start(bf16[128,1024]{1,0:T(8,128)(2,1)S(1)} %convolution_convert_fusion.3), channel_id=1, source_target_pairs={{0,3},{1,0},{2,1},{3,2},{4,7},{5,4},{6,5},{7,6},{8,11},{9,8},{10,9... | collective-permute-start | bytes 786440 | tf_op jit(solution)/shard_map/ppermute | solution.py:17
  71.8 14.4 %collective-permute-start.1 = (bf16[128,1024]{1,0:T(8,128)(2,1)S(1)}, bf16[128,1024]{1,0:T(8,128)(2,1)S(1)}, u32[]{:S(2)}, u32[]{:S(2)}) collective-permute-start(bf16[128,1024]{1,0:T(8,128)(2,1)S(1)} %convolution_convert_fusion.7), channel_id=1, source_target_pairs={{0,1},{1,2},{2,3},{3,0},{4,5},{5,6},{6,7},{7,4},{8,9},{9,10},{10,1... | collective-permute-start | bytes 786440 | tf_op jit(solution)/shard_map/ppermute | solution.py:17
  86.7 27.6 %collective-permute-start.3 = (bf16[256,1024]{1,0:T(8,128)(2,1)S(1)}, bf16[256,1024]{1,0:T(8,128)(2,1)S(1)}, u32[]{:S(2)}, u32[]{:S(2)}) collective-permute-start(bf16[256,1024]{1,0:T(8,128)(2,1)S(1)} %pad_maximum_fusion.6), channel_id=1, source_target_pairs={{0,1},{1,2},{2,3},{3,0},{4,5},{5,6},{6,7},{7,4},{8,9},{9,10},{10,1... | collective-permute-start | bytes 1572872 | tf_op jit(solution)/shard_map/ppermute | solution.py:17
  92.3 28.0 %collective-permute-start.4 = (bf16[256,1024]{1,0:T(8,128)(2,1)S(1)}, bf16[256,1024]{1,0:T(8,128)(2,1)S(1)}, u32[]{:S(2)}, u32[]{:S(2)}) collective-permute-start(bf16[256,1024]{1,0:T(8,128)(2,1)S(1)} %pad_maximum_fusion.7), channel_id=1, source_target_pairs={{0,3},{1,0},{2,1},{3,2},{4,7},{5,4},{6,5},{7,6},{8,11},{9,8},{10,9... | collective-permute-start | bytes 1572872 | tf_op jit(solution)/shard_map/ppermute | solution.py:17

commit v3 on v2

--- a/solution.py
+++ b/solution.py
@@ -88,7 +88,7 @@
     core = lax.axis_index("core")
     panels = panel_slots[0].reshape(NPAN, -1, depth)
     owner, owner_next = owners[0], owners[1]
-    owned = jnp.where(lax.axis_index(COL) == owner, panels[0], panels[1])
+    owned = pick(panels, jnp.where(lax.axis_index(COL) == owner, 0, 1))
     got = spread_pieces(owned)
     right = g2_block.transpose(1, 0, 2).reshape(-1, width)
     got, right = lax.optimization_barrier((got, right))

time: 124 us -> 124 us (level)
  other arithmetic: 5.05 us -> 3 us
  local copies, waits for them, and re-layouts: 7.99 us -> 9.87 us
    select_n x1 -> x0, other arithmetic: 2.05 us -> none  [shards(): owned = jnp.where(lax.axis_index(COL) == owner, panels[0], panels[1])]
    dynamic_slice x1 -> x2, local copies, waits for them, and re-layouts: 0.01 us -> 1.87 us  [pick(): return lax.dynamic_index_in_dim(array, index, 0, keepdims=False)]
where the time goes in v3:
time: 124 us; the launch traced here: 123 us
  waiting for transfers between devices  58.1 us (47%)
  starting transfers between devices  37 us (30%)
  local copies, waits for them, and re-layouts  9.87 us (8%)
  matrix products  9.24 us (7%)
  between operations  6.1 us (5%)
  other arithmetic  3 us (2%)
    ppermute x4, waiting for transfers between devices, shift(): lax.ppermute(array, 'row', [(index, (index + step) % size) for index in r...  29.3 us
    all_to_all x1, waiting for transfers between devices, gather(): own = lax.all_to_all(copies, ('y', 'z', 'x'), 0, 0, tiled=True)  16 us
    ppermute x4, starting transfers between devices, shift(): lax.ppermute(array, 'row', [(index, (index + step) % size) for index in r...  15.6 us
    all_to_all x1, starting transfers between devices, spread_pieces(): return lax.all_to_all(pieces, COL, 0, 0, tiled=True)  13.9 us
    all_to_all x1, waiting for transfers between devices, spread_pieces(): return lax.all_to_all(pieces, COL, 0, 0, tiled=True)  11.1 us
    all_to_all x1, starting transfers between devices, gather(): own = lax.all_to_all(copies, ('y', 'z', 'x'), 0, 0, tiled=True)  5.55 us
    unnamed x7, local copies, waits for them, and re-layouts  4.89 us
    dot_general x8, matrix products, term(): jnp.dot(left, right, preferred_element_type=jnp.float32)  3.62 us
  transfers between devices with their start and end apart: 7, of which 7 were waited for; matrix products, arithmetic and copies ran while one was open for 9% of the time, Pallas kernels for 0%

profile of v3, /device:TPU:112, one launch (start us, length us, event | category | flops | bytes accessed | tf_op | source)
XLA Modules:
  0.0 123.2 jit_solution(10055342507919338043)
XLA Ops:
  0.0 1.4 %fusion.67 = (s32[1]{0:T(128)}, s32[1]{0:T(128)}) fusion(s32[2]{0:T(128)} %param.8), kind=kLoop, calls=%fused_computation.111 | loop fusion | bytes 16 | tf_op jit(solution)/shard_map/slice | solution.py:90
  3.3 1.9 %constant_dynamic-slice_fusion.1 = bf16[1,512,512]{2,1,0:T(8,128)(2,1)} fusion(bf16[2,512,512]{2,1,0:T(8,128)(2,1)} %bitcast.145, s32[]{:T(128)S(6)} %select_n.139), kind=kLoop, calls=%fused_computation.100 | loop fusion | bytes 1048580 | tf_op jit(solution)/shard_map/jit(dynamic_index_in_dim)/dynamic_slice | solution.py:12
  5.2 13.9 %all-to-all-start.1 = ((bf16[128,8,256]{2,1,0:T(8,128)(2,1)}), bf16[128,8,256]{2,1,0:T(8,128)(2,1)S(1)}, u32[]{:S(2)}, u32[]{:S(2)}) async-start(bf16[128,8,256]{2,1,0:T(8,128)(2,1)} %bitcast.8), calls=%async_computation.1 | async-start | bytes 1048576 | tf_op jit(solution)/shard_map/all_to_all | solution.py:23
  21.6 3.5 %copy.14 = bf16[512,2,1024]{2,0,1:T(8,128)(2,1)} copy(bf16[512,2,1024]{2,1,0:T(2,128)(2,1)} %param.6) | data formatting | bytes 4194304 | tf_op args[0]
  26.5 11.1 %all-to-all-done.1 = bf16[128,8,256]{2,1,0:T(8,128)(2,1)S(1)} async-done(((bf16[128,8,256]{2,1,0:T(8,128)(2,1)}), bf16[128,8,256]{2,1,0:T(8,128)(2,1)S(1)}, u32[]{:S(2)}, u32[]{:S(2)}) %all-to-all-start.1) | async-done | bytes 524320 | tf_op jit(solution)/shard_map/all_to_all | solution.py:23
  37.6 0.8 broadcast_in_dim.2
  38.4 5.6 %all-to-all-start.2 = ((bf16[64,2,8,256]{3,2,1,0:T(8,128)(2,1)}), bf16[64,2,8,256]{3,2,1,0:T(8,128)(2,1)S(1)}, u32[]{:S(2)}, u32[]{:S(2)}) async-start(bf16[64,2,8,256]{3,2,1,0:T(8,128)(2,1)} %broadcast_in_dim.2), calls=%async_computation.2 | async-start | bytes 1048576 | tf_op jit(solution)/shard_map/all_to_all | solution.py:29
  44.1 0.1 fusion.62
  44.1 0.1 div.24
  44.2 0.1 rem.126
  44.3 16.0 %all-to-all-done.2 = bf16[64,2,8,256]{3,2,1,0:T(8,128)(2,1)S(1)} async-done(((bf16[64,2,8,256]{3,2,1,0:T(8,128)(2,1)}), bf16[64,2,8,256]{3,2,1,0:T(8,128)(2,1)S(1)}, u32[]{:S(2)}, u32[]{:S(2)}) %all-to-all-start.2) | async-done | bytes 524320 | tf_op jit(solution)/shard_map/all_to_all | solution.py:29
  60.3 1.9 %collective-permute-start = (bf16[64,2,8,256]{3,2,1,0:T(8,128)(2,1)S(1)}, bf16[64,2,8,256]{3,2,1,0:T(8,128)(2,1)S(1)}, u32[]{:S(2)}, u32[]{:S(2)}) collective-permute-start(bf16[64,2,8,256]{3,2,1,0:T(8,128)(2,1)S(1)} %all-to-all-done.2), channel_id=1, source_target_pairs={{0,4},{4,0},{1,5},{5,1},{2,6},{6,2},{3,7},{7,3},{8,12},{12,8},{9,1... | collective-permute-start | bytes 1572872 | tf_op jit(solution)/shard_map/ppermute | solution.py:30
  62.2 0.1 sign_compare_fusion.1
  62.3 0.1 ne.109
  62.4 1.7 %collective-permute-done = bf16[64,2,8,256]{3,2,1,0:T(8,128)(2,1)S(1)} collective-permute-done((bf16[64,2,8,256]{3,2,1,0:T(8,128)(2,1)S(1)}, bf16[64,2,8,256]{3,2,1,0:T(8,128)(2,1)S(1)}, u32[]{:S(2)}, u32[]{:S(2)}) %collective-permute-start) | collective-permute-done | bytes 524320 | tf_op jit(solution)/shard_map/ppermute | solution.py:30
  64.1 0.1 select_bitcast_fusion.2
  64.2 0.2 fusion.64
  64.4 0.1 pad_maximum_fusion.2
  64.5 0.1 pad_maximum_fusion
  64.6 1.3 %copy-done.1 = bf16[512,2,1024]{2,0,1:T(8,128)(2,1)S(1)} copy-done((bf16[512,2,1024]{2,0,1:T(8,128)(2,1)S(1)}, bf16[512,2,1024]{2,0,1:T(8,128)(2,1)}, u32[]{:S(2)}) %copy-start.1) | copy-done | bytes 2097176
  66.0 0.4 convolution_convert_fusion.4
  66.4 0.4 convolution_convert_fusion.7
  66.9 0.1 pad_maximum_fusion.4
  67.0 0.1 pad_maximum_fusion.1
  67.1 0.4 convolution_convert_fusion.3
  67.6 4.0 %collective-permute-start.2 = (bf16[128,1024]{1,0:T(8,128)(2,1)S(1)}, bf16[128,1024]{1,0:T(8,128)(2,1)S(1)}, u32[]{:S(2)}, u32[]{:S(2)}) collective-permute-start(bf16[128,1024]{1,0:T(8,128)(2,1)S(1)} %convolution_convert_fusion.3), channel_id=1, source_target_pairs={{0,3},{1,0},{2,1},{3,2},{4,7},{5,4},{6,5},{7,6},{8,11},{9,8},{10,9... | collective-permute-start | bytes 786440 | tf_op jit(solution)/shard_map/ppermute | solution.py:17
  71.6 3.9 %collective-permute-start.1 = (bf16[128,1024]{1,0:T(8,128)(2,1)S(1)}, bf16[128,1024]{1,0:T(8,128)(2,1)S(1)}, u32[]{:S(2)}, u32[]{:S(2)}) collective-permute-start(bf16[128,1024]{1,0:T(8,128)(2,1)S(1)} %convolution_convert_fusion.7), channel_id=1, source_target_pairs={{0,1},{1,2},{2,3},{3,0},{4,5},{5,6},{6,7},{7,4},{8,9},{9,10},{10,1... | collective-permute-start | bytes 786440 | tf_op jit(solution)/shard_map/ppermute | solution.py:17
  75.6 0.4 convolution_convert_fusion.5
  76.0 8.7 %collective-permute-done.2 = bf16[128,1024]{1,0:T(8,128)(2,1)S(1)} collective-permute-done((bf16[128,1024]{1,0:T(8,128)(2,1)S(1)}, bf16[128,1024]{1,0:T(8,128)(2,1)S(1)}, u32[]{:S(2)}, u32[]{:S(2)}) %collective-permute-start.2) | collective-permute-done | bytes 262176 | tf_op jit(solution)/shard_map/ppermute | solution.py:17
  84.7 0.4 add_convert_fusion
  85.2 0.8 collective-permute-done.1
  86.0 0.4 add_convert_fusion.1
  86.5 5.5 %collective-permute-start.3 = (bf16[256,1024]{1,0:T(8,128)(2,1)S(1)}, bf16[256,1024]{1,0:T(8,128)(2,1)S(1)}, u32[]{:S(2)}, u32[]{:S(2)}) collective-permute-start(bf16[256,1024]{1,0:T(8,128)(2,1)S(1)} %pad_maximum_fusion.6), channel_id=1, source_target_pairs={{0,1},{1,2},{2,3},{3,0},{4,5},{5,6},{6,7},{7,4},{8,9},{9,10},{10,1... | collective-permute-start | bytes 1572872 | tf_op jit(solution)/shard_map/ppermute | solution.py:17
  92.1 2.1 %collective-permute-start.4 = (bf16[256,1024]{1,0:T(8,128)(2,1)S(1)}, bf16[256,1024]{1,0:T(8,128)(2,1)S(1)}, u32[]{:S(2)}, u32[]{:S(2)}) collective-permute-start(bf16[256,1024]{1,0:T(8,128)(2,1)S(1)} %pad_maximum_fusion.7), channel_id=1, source_target_pairs={{0,3},{1,0},{2,1},{3,2},{4,7},{5,4},{6,5},{7,6},{8,11},{9,8},{10,9... | collective-permute-start | bytes 1572872 | tf_op jit(solution)/shard_map/ppermute | solution.py:17
  94.2 1.7 %convolution_bitcast_fusion.1 = f32[2,128,400]{1,2,0:T(8,128)S(1)} fusion(f32[2,400,400]{2,1,0:T(8,128)S(1)} %copy-done, s32[128]{0:T(128)S(1)} %get-tuple-element.46), kind=kOutput, calls=%fused_computation.8 | convolution fusion | flops 491571200 | bytes 1690112 | tf_op jit(solution)/shard_map/qi,cik->cqk/dot_general | solution.py:75
  96.0 1.7 %convolution_bitcast_fusion = f32[2,128,400]{1,2,0:T(8,128)S(1)} fusion(f32[2,400,400]{2,1,0:T(8,128)S(1)} %copy-done, s32[128]{0:T(128)S(1)} %get-tuple-element.47), kind=kOutput, calls=%fused_computation.7 | convolution fusion | flops 491571200 | bytes 1690112 | tf_op jit(solution)/shard_map/qi,cik->cqk/dot_general | solution.py:75
  97.7 1.1 fusion.1
  98.8 1.1 fusion.4
  99.9 0.2 multiply_subtract_fusion
  100.3 13.8 %collective-permute-done.3 = bf16[256,1024]{1,0:T(8,128)(2,1)S(1)} collective-permute-done((bf16[256,1024]{1,0:T(8,128)(2,1)S(1)}, bf16[256,1024]{1,0:T(8,128)(2,1)S(1)}, u32[]{:S(2)}, u32[]{:S(2)}) %collective-permute-start.3) | collective-permute-done | bytes 524320 | tf_op jit(solution)/shard_map/ppermute | solution.py:17
  114.1 0.1 convert_element_type.84
  114.2 5.9 %collective-permute-done.4 = bf16[256,1024]{1,0:T(8,128)(2,1)S(1)} collective-permute-done((bf16[256,1024]{1,0:T(8,128)(2,1)S(1)}, bf16[256,1024]{1,0:T(8,128)(2,1)S(1)}, u32[]{:S(2)}, u32[]{:S(2)}) %collective-permute-start.4) | collective-permute-done | bytes 524320 | tf_op jit(solution)/shard_map/ppermute | solution.py:17
  120.1 0.1 convert_element_type.85
  120.3 0.5 fusion.15
  120.7 0.3 copy.19
  121.0 0.5 fusion.13
  121.5 0.3 copy.20
  121.8 1.5 %maximum_bitcast_fusion.1 = bf16[64,2,2,1024]{3,2,1,0:T(2,128)(2,1)} fusion(bf16[1,2,64,1024]{3,1,0,2:T(2,128)(2,1)S(1)} %copy.20, bf16[1,2,64,1024]{3,1,0,2:T(2,128)(2,1)S(1)} %copy.19), kind=kLoop, calls=%fused_computation.44 | loop fusion | flops 262144 | bytes 1048576 | tf_op jit(solution)/shard_map/transpose | solution.py:111
  (17 shorter events, 0.3 us)
Async XLA Ops:
  0.0 94.2 %copy-start = (f32[2,400,400]{2,1,0:T(8,128)S(1)}, f32[2,400,400]{2,1,0:T(8,128)}, u32[]{:S(2)}) copy-start(f32[2,400,400]{2,1,0:T(8,128)} %param.9) | copy-start | bytes 3840004
  5.2 32.4 %all-to-all-start.1 = ((bf16[128,8,256]{2,1,0:T(8,128)(2,1)}), bf16[128,8,256]{2,1,0:T(8,128)(2,1)S(1)}, u32[]{:S(2)}, u32[]{:S(2)}) async-start(bf16[128,8,256]{2,1,0:T(8,128)(2,1)} %bitcast.8), calls=%async_computation.1 | async-start | bytes 1048576 | tf_op jit(solution)/shard_map/all_to_all | solution.py:23
  21.6 22.4 %copy-start.2 = (s32[2]{0:T(128)S(1)}, s32[2]{0:T(128)}, u32[]{:S(2)}) copy-start(s32[2]{0:T(128)} %param.8) | copy-start | bytes 28
  38.4 21.9 %all-to-all-start.2 = ((bf16[64,2,8,256]{3,2,1,0:T(8,128)(2,1)}), bf16[64,2,8,256]{3,2,1,0:T(8,128)(2,1)S(1)}, u32[]{:S(2)}, u32[]{:S(2)}) async-start(bf16[64,2,8,256]{3,2,1,0:T(8,128)(2,1)} %broadcast_in_dim.2), calls=%async_computation.2 | async-start | bytes 1048576 | tf_op jit(solution)/shard_map/all_to_all | solution.py:29
  60.3 3.8 %collective-permute-start = (bf16[64,2,8,256]{3,2,1,0:T(8,128)(2,1)S(1)}, bf16[64,2,8,256]{3,2,1,0:T(8,128)(2,1)S(1)}, u32[]{:S(2)}, u32[]{:S(2)}) collective-permute-start(bf16[64,2,8,256]{3,2,1,0:T(8,128)(2,1)S(1)} %all-to-all-done.2), channel_id=1, source_target_pairs={{0,4},{4,0},{1,5},{5,1},{2,6},{6,2},{3,7},{7,3},{8,12},{12,8},{9,1... | collective-permute-start | bytes 1572872 | tf_op jit(solution)/shard_map/ppermute | solution.py:30
  64.4 1.6 %copy-start.1 = (bf16[512,2,1024]{2,0,1:T(8,128)(2,1)S(1)}, bf16[512,2,1024]{2,0,1:T(8,128)(2,1)}, u32[]{:S(2)}) copy-start(bf16[512,2,1024]{2,0,1:T(8,128)(2,1)} %copy.14) | copy-start | bytes 6291460
  67.6 17.1 %collective-permute-start.2 = (bf16[128,1024]{1,0:T(8,128)(2,1)S(1)}, bf16[128,1024]{1,0:T(8,128)(2,1)S(1)}, u32[]{:S(2)}, u32[]{:S(2)}) collective-permute-start(bf16[128,1024]{1,0:T(8,128)(2,1)S(1)} %convolution_convert_fusion.3), channel_id=1, source_target_pairs={{0,3},{1,0},{2,1},{3,2},{4,7},{5,4},{6,5},{7,6},{8,11},{9,8},{10,9... | collective-permute-start | bytes 786440 | tf_op jit(solution)/shard_map/ppermute | solution.py:17
  71.6 14.4 %collective-permute-start.1 = (bf16[128,1024]{1,0:T(8,128)(2,1)S(1)}, bf16[128,1024]{1,0:T(8,128)(2,1)S(1)}, u32[]{:S(2)}, u32[]{:S(2)}) collective-permute-start(bf16[128,1024]{1,0:T(8,128)(2,1)S(1)} %convolution_convert_fusion.7), channel_id=1, source_target_pairs={{0,1},{1,2},{2,3},{3,0},{4,5},{5,6},{6,7},{7,4},{8,9},{9,10},{10,1... | collective-permute-start | bytes 786440 | tf_op jit(solution)/shard_map/ppermute | solution.py:17
  86.5 27.6 %collective-permute-start.3 = (bf16[256,1024]{1,0:T(8,128)(2,1)S(1)}, bf16[256,1024]{1,0:T(8,128)(2,1)S(1)}, u32[]{:S(2)}, u32[]{:S(2)}) collective-permute-start(bf16[256,1024]{1,0:T(8,128)(2,1)S(1)} %pad_maximum_fusion.6), channel_id=1, source_target_pairs={{0,1},{1,2},{2,3},{3,0},{4,5},{5,6},{6,7},{7,4},{8,9},{9,10},{10,1... | collective-permute-start | bytes 1572872 | tf_op jit(solution)/shard_map/ppermute | solution.py:17
  92.1 28.0 %collective-permute-start.4 = (bf16[256,1024]{1,0:T(8,128)(2,1)S(1)}, bf16[256,1024]{1,0:T(8,128)(2,1)S(1)}, u32[]{:S(2)}, u32[]{:S(2)}) collective-permute-start(bf16[256,1024]{1,0:T(8,128)(2,1)S(1)} %pad_maximum_fusion.7), channel_id=1, source_target_pairs={{0,3},{1,0},{2,1},{3,2},{4,7},{5,4},{6,5},{7,6},{8,11},{9,8},{10,9... | collective-permute-start | bytes 1572872 | tf_op jit(solution)/shard_map/ppermute | solution.py:17
